TPU v7x, 32 devices: a whole 2x2x4 slice. The times are simulated.
32 devices in a mesh: ctx: 8 (over y, x, core), section: 4 (over z).
Axes of the slice: x: 2, y: 2, z: 4, core: 2. Of those that a mesh axis runs over, the one named last changes fastest.
Arguments:
- queries: bfloat16 [4, 2048, 2048], P('section', 'ctx'), may hold values from -9 to 9
- keys: bfloat16 [4, 2048, 2048], P('section', 'ctx'), may hold values from -9 to 9
- values: bfloat16 [4, 2048, 2048], P('section', 'ctx'), may hold values from -6 to 6
- segments: int32 [4, 2048], replicated, may hold values from 0 to 1, as said below
- gain_query: bfloat16 [4, 2048], P('section'), may hold values from 0.099609375 to 1.8984375
- gain_key: bfloat16 [4, 2048], P('section'), may hold values from 0.099609375 to 1.8984375
Outputs:
- mixed: bfloat16 [4, 2048, 2048], P('section', 'ctx')
Inputs may be any that keep to these rules, and one draw needn't show every extreme that they name: `segments`: along the events of a micro-batch the ids never fall and each of the two ids 0, 1 is used.
All inputs are finite; a program needn't handle non-finite values.
Results may differ from a plain program's by a relative error of at most 0.004.
The roundings to bfloat16 on the way count: a program that leaves them out, or rounds other values in their place, can miss the bound.
Values may be sent and summed in bfloat16 or wider, within the bound.
A program may use at most 64 MiB of HBM per device.

v0:
```python
import math

import jax
import jax.numpy as jnp
from jax import lax
from jax.sharding import PartitionSpec as P

HD = 128
HOPS = 3
WINDOW = 768


NEG = -1e30


def from_behind(block, axis, distance):
    devices = range(lax.axis_size(axis))
    route = [(i - distance, i) for i in devices if i - distance in devices]
    return lax.ppermute(block, axis, route)


def shifted(block, axis, distance):
    devices = range(lax.axis_size(axis))
    route = [((i - distance) % len(devices), i) for i in devices]
    return lax.ppermute(block, axis, route)


def tile_scores(query_g, key_tile):

    def compute():
        return jnp.einsum("qhd,khd->hqk", query_g, key_tile, preferred_element_type=jnp.float32)

    return compute()


def tile_values(prob_tile, value_tile):

    def compute():
        return jnp.einsum("hqk,khd->qhd", prob_tile, value_tile, preferred_element_type=jnp.float32)

    return compute()


def head_attention(queries, key_tiles, value_tiles, allowed, score_scale):
    row_count = queries.shape[0]
    full_width = queries.shape[1]
    head_count = full_width // HD
    per_group = min(4, head_count)
    group_count = head_count // per_group
    tile_count = key_tiles.shape[0]

    def one_group(group_index):
        offset = group_index * per_group * HD
        query_g = lax.dynamic_slice_in_dim(queries, offset, per_group * HD, 1).reshape(
            row_count, per_group, HD
        )
        key_g = lax.dynamic_slice_in_dim(key_tiles, offset, per_group * HD, 2).reshape(
            tile_count, row_count, per_group, HD
        )
        value_g = lax.dynamic_slice_in_dim(value_tiles, offset, per_group * HD, 2).reshape(
            tile_count, row_count, per_group, HD
        )
        pieces = []
        for j in range(tile_count):
            pieces.append(tile_scores(query_g, key_g[j]))
        scores = jnp.concatenate(pieces, axis=2) * score_scale
        scores = jnp.where(allowed[None], scores, NEG)
        row_max = jnp.max(scores, axis=2, keepdims=True)
        probs = jnp.where(allowed[None], jnp.exp(scores - row_max), 0.0)
        row_total = jnp.sum(probs, axis=2)
        rounded = probs.astype(jnp.bfloat16)
        summed = jnp.zeros((row_count, per_group, HD), jnp.float32)
        for j in range(tile_count):
            prob_tile = rounded[:, :, j * row_count : (j + 1) * row_count]
            summed = summed + tile_values(prob_tile, value_g[j])
        result = summed / jnp.transpose(row_total)[:, :, None]
        return result.reshape(row_count, per_group * HD).astype(jnp.bfloat16)

    stacked = lax.map(one_group, jnp.arange(group_count, dtype=jnp.int32))
    return jnp.transpose(stacked, (1, 0, 2)).reshape(row_count, full_width)


def fetch_prior(paired, layer_name):
    blocks = []
    if layer_name == "first":
        current = paired
        for hop in range(HOPS):
            current = from_behind(current, "ctx", 1)
            blocks.append(current)
    else:
        current = paired
        for hop in range(HOPS):
            current = from_behind(current, "ctx", 1)
            blocks.append(current)
    return blocks


def attention_layer(queries, keys, values, segrow, score_scale, layer_name):
    row_count = queries.shape[0]
    ctx_index = lax.axis_index("ctx")
    paired = jnp.stack([keys, values])
    blocks = fetch_prior(paired, layer_name)
    ordered = jnp.stack(blocks[::-1] + [paired])
    key_tiles = ordered[:, 0]
    value_tiles = ordered[:, 1]
    padded_seg = jnp.concatenate([jnp.full((HOPS * row_count,), -1, jnp.int32), segrow])
    key_seg = lax.dynamic_slice_in_dim(padded_seg, ctx_index * row_count, (HOPS + 1) * row_count, 0)
    query_seg = lax.dynamic_slice_in_dim(segrow, ctx_index * row_count, row_count, 0)
    query_pos = ctx_index * row_count + jnp.arange(row_count, dtype=jnp.int32)
    key_pos = (ctx_index - HOPS) * row_count + jnp.arange((HOPS + 1) * row_count, dtype=jnp.int32)
    allowed = (
        (query_seg[:, None] == key_seg[None, :])
        & (key_pos[None, :] <= query_pos[:, None])
        & (key_pos[None, :] > query_pos[:, None] - WINDOW)
        & (key_seg[None, :] >= 0)
    )
    return head_attention(queries, key_tiles, value_tiles, allowed, score_scale)


def per_device(queries, keys, values, segments, gain_query, gain_key):
    section_index = lax.axis_index("section")
    section_count = lax.axis_size("section")
    own_seg = lax.dynamic_index_in_dim(segments, section_index, 0, keepdims=False)
    prior_index = (section_index + section_count - 1) % section_count
    prior_seg = lax.dynamic_index_in_dim(segments, prior_index, 0, keepdims=False)
    first_local = attention_layer(
        queries[0], keys[0], values[0], own_seg, 1.0 / math.sqrt(HD), "first"
    )
    received = shifted(first_local, "section", 1)
    shaped = received.astype(jnp.float32).reshape(received.shape[0], -1, HD)
    mean_square = jnp.mean(shaped * shaped, axis=2, keepdims=True)
    normed = (shaped * lax.rsqrt(mean_square + 1e-06)).reshape(received.shape).astype(jnp.bfloat16)
    normed_f = normed.astype(jnp.float32)
    query_two = (normed_f * gain_query.astype(jnp.float32)).astype(jnp.bfloat16)
    key_two = (normed_f * gain_key.astype(jnp.float32)).astype(jnp.bfloat16)
    second = attention_layer(query_two, key_two, normed, prior_seg, 1.0 / HD, "second")
    mixed = (second.astype(jnp.float32) + normed_f).astype(jnp.bfloat16)
    return mixed[None]


def solution(mesh):
    return jax.shard_map(
        per_device,
        mesh=mesh,
        in_specs=(
            P("section", "ctx", None),
            P("section", "ctx", None),
            P("section", "ctx", None),
            P(),
            P("section", None),
            P("section", None),
        ),
        out_specs=P("section", "ctx", None),
        check_vma=False,
    )
```

profile of v0, /device:TPU:1, one launch (start us, length us, event | category | flops | bytes accessed | tf_op | source)
XLA Modules:
  0.0 391.1 jit_solution(8759230896435558578)
XLA Ops:
  0.0 1.4 constant_dynamic-update-slice_fusion.3
  1.6 4.5 %collective-permute-start = (bf16[2,256,2048]{2,1,0:T(8,128)(2,1)S(1)}, bf16[2,256,2048]{2,1,0:T(8,128)(2,1)S(1)}, u32[]{:S(2)}, u32[]{:S(2)}) collective-permute-start(bf16[2,256,2048]{2,1,0:T(8,128)(2,1)S(1)} %constant_dynamic-update-slice_fusion.2), channel_id=1, source_target_pairs={{0,4},{4,8},{8,12},{12,16},{16,20},{20,24},{24,28},{1,5},{5,9},{9,... | collective-permute-start | bytes 6291464 | tf_op jit(solution)/shard_map/ppermute | solution.py:19
  6.2 23.0 %collective-permute-done = bf16[2,256,2048]{2,1,0:T(8,128)(2,1)S(1)} collective-permute-done((bf16[2,256,2048]{2,1,0:T(8,128)(2,1)S(1)}, bf16[2,256,2048]{2,1,0:T(8,128)(2,1)S(1)}, u32[]{:S(2)}, u32[]{:S(2)}) %collective-permute-start) | collective-permute-done | bytes 2097184 | tf_op jit(solution)/shard_map/ppermute | solution.py:19
  30.5 4.4 %collective-permute-start.1 = (bf16[2,256,2048]{2,1,0:T(8,128)(2,1)S(1)}, bf16[2,256,2048]{2,1,0:T(8,128)(2,1)}, u32[]{:S(2)}, u32[]{:S(2)}) collective-permute-start(bf16[2,256,2048]{2,1,0:T(8,128)(2,1)S(1)} %collective-permute-done), channel_id=1, source_target_pairs={{0,4},{4,8},{8,12},{12,16},{16,20},{20,24},{24,28},{1,5},{5,9},{9,... | collective-permute-start | bytes 6291464 | tf_op jit(solution)/shard_map/ppermute | solution.py:19
  34.8 23.0 %collective-permute-done.1 = bf16[2,256,2048]{2,1,0:T(8,128)(2,1)} collective-permute-done((bf16[2,256,2048]{2,1,0:T(8,128)(2,1)S(1)}, bf16[2,256,2048]{2,1,0:T(8,128)(2,1)}, u32[]{:S(2)}, u32[]{:S(2)}) %collective-permute-start.1) | collective-permute-done | bytes 2097184 | tf_op jit(solution)/shard_map/ppermute | solution.py:19
  57.8 4.5 %collective-permute-start.2 = (bf16[2,256,2048]{2,1,0:T(8,128)(2,1)}, bf16[2,256,2048]{2,1,0:T(8,128)(2,1)}, u32[]{:S(2)}, u32[]{:S(2)}) collective-permute-start(bf16[2,256,2048]{2,1,0:T(8,128)(2,1)} %collective-permute-done.1), channel_id=1, source_target_pairs={{0,4},{4,8},{8,12},{12,16},{16,20},{20,24},{24,28},{1,5},{5,9},{9,... | collective-permute-start | bytes 6291464 | tf_op jit(solution)/shard_map/ppermute | solution.py:19
  62.3 1.3 copy.119
  63.9 21.7 %collective-permute-done.2 = bf16[2,256,2048]{2,1,0:T(8,128)(2,1)} collective-permute-done((bf16[2,256,2048]{2,1,0:T(8,128)(2,1)}, bf16[2,256,2048]{2,1,0:T(8,128)(2,1)}, u32[]{:S(2)}, u32[]{:S(2)}) %collective-permute-start.2) | collective-permute-done | bytes 2097184 | tf_op jit(solution)/shard_map/ppermute | solution.py:19
  85.6 3.8 pad_maximum_fusion
  89.4 3.8 slice_bitcast_fusion.2
  94.3 81.6 %while.26 = (s32[]{:T(128)}, bf16[4,256,512]{1,2,0:T(8,128)(2,1)}, s32[4]{0:T(128)S(1)}, bf16[4,256,2048]{2,1,0:T(8,128)(2,1)}, bf16[256,2048]{0,1:T(8,128)(2,1)...) while((s32[]{:T(128)}, bf16[4,256,512]{1,2,0:T(8,128)(2,1)}, ...), condition=%wide.region_3.4_spmd.clone, body=%wide.region_0.3_spmd.clone.sunk | while | flops 548537344 | bytes 30167868 | solution.py:79
  95.5 2.6 constant_dynamic-slice_fusion.24
  103.9 4.7 %fusion.144 = (f32[4,256]{1,0:T(4,128)S(1)}, bf16[4,256,1024]{1,2,0:T(8,128)(2,1)S(1)}) fusion(f32[4,256,256]{1,2,0:T(8,128)S(1)} %fusion.140, f32[4,256,256]{1,2,0:T(8,128)} %fusion.141, f32[4,256,256]{1,2,0:T(8,128)} %fusion.142, f32[4,256,256]{1,2,0:T(8,128)S(1)} %fusion.143, pred[256,1024]{0,1:T(8,128)(4,1)S(1)} %and_and_fusion.4), kind=kOutput, calls=%fused_computation.94.clone.1 | output fusion | flops 9438207 | bytes 6557696 | tf_op jit(solution)/shard_map/while/body/eval_jaxpr/sub | solution.py:69
  115.9 2.6 constant_dynamic-slice_fusion.24
  120.1 1.3 fusion.141
  124.3 4.7 %fusion.144 = (f32[4,256]{1,0:T(4,128)S(1)}, bf16[4,256,1024]{1,2,0:T(8,128)(2,1)S(1)}) fusion(f32[4,256,256]{1,2,0:T(8,128)S(1)} %fusion.140, f32[4,256,256]{1,2,0:T(8,128)} %fusion.141, f32[4,256,256]{1,2,0:T(8,128)} %fusion.142, f32[4,256,256]{1,2,0:T(8,128)S(1)} %fusion.143, pred[256,1024]{0,1:T(8,128)(4,1)S(1)} %and_and_fusion.4), kind=kOutput, calls=%fused_computation.94.clone.1 | output fusion | flops 9438207 | bytes 6557696 | tf_op jit(solution)/shard_map/while/body/eval_jaxpr/sub | solution.py:69
  136.3 2.6 constant_dynamic-slice_fusion.24
  140.5 1.3 fusion.141
  144.7 4.7 %fusion.144 = (f32[4,256]{1,0:T(4,128)S(1)}, bf16[4,256,1024]{1,2,0:T(8,128)(2,1)S(1)}) fusion(f32[4,256,256]{1,2,0:T(8,128)S(1)} %fusion.140, f32[4,256,256]{1,2,0:T(8,128)} %fusion.141, f32[4,256,256]{1,2,0:T(8,128)} %fusion.142, f32[4,256,256]{1,2,0:T(8,128)S(1)} %fusion.143, pred[256,1024]{0,1:T(8,128)(4,1)S(1)} %and_and_fusion.4), kind=kOutput, calls=%fused_computation.94.clone.1 | output fusion | flops 9438207 | bytes 6557696 | tf_op jit(solution)/shard_map/while/body/eval_jaxpr/sub | solution.py:69
  156.7 2.6 constant_dynamic-slice_fusion.24
  160.9 1.3 fusion.141
  165.1 4.7 %fusion.144 = (f32[4,256]{1,0:T(4,128)S(1)}, bf16[4,256,1024]{1,2,0:T(8,128)(2,1)S(1)}) fusion(f32[4,256,256]{1,2,0:T(8,128)S(1)} %fusion.140, f32[4,256,256]{1,2,0:T(8,128)} %fusion.141, f32[4,256,256]{1,2,0:T(8,128)} %fusion.142, f32[4,256,256]{1,2,0:T(8,128)S(1)} %fusion.143, pred[256,1024]{0,1:T(8,128)(4,1)S(1)} %and_and_fusion.4), kind=kOutput, calls=%fused_computation.94.clone.1 | output fusion | flops 9438207 | bytes 6557696 | tf_op jit(solution)/shard_map/while/body/eval_jaxpr/sub | solution.py:69
  175.9 1.5 copy.153
  177.4 1.4 collective-permute-start.3
  178.8 14.1 %collective-permute-done.3 = bf16[256,2048]{1,0:T(8,128)(2,1)S(1)} collective-permute-done((bf16[256,2048]{1,0:T(8,128)(2,1)S(1)}, bf16[256,2048]{1,0:T(8,128)(2,1)S(1)}, u32[]{:S(2)}, u32[]{:S(2)}) %collective-permute-start.3) | collective-permute-done | bytes 1048608 | tf_op jit(solution)/shard_map/ppermute | solution.py:25
  195.0 2.0 fusion.37
  198.0 16.7 %collective-permute-start.4 = (bf16[2,256,2048]{2,1,0:T(8,128)(2,1)S(1)}, bf16[2,256,2048]{2,1,0:T(8,128)(2,1)S(1)}, u32[]{:S(2)}, u32[]{:S(2)}) collective-permute-start(bf16[2,256,2048]{2,1,0:T(8,128)(2,1)S(1)} %get-tuple-element.421), channel_id=1, source_target_pairs={{0,4},{4,8},{8,12},{12,16},{16,20},{20,24},{24,28},{1,5},{5,9},{9,... | collective-permute-start | bytes 6291464 | tf_op jit(solution)/shard_map/ppermute | solution.py:19
  214.7 23.0 %collective-permute-done.4 = bf16[2,256,2048]{2,1,0:T(8,128)(2,1)S(1)} collective-permute-done((bf16[2,256,2048]{2,1,0:T(8,128)(2,1)S(1)}, bf16[2,256,2048]{2,1,0:T(8,128)(2,1)S(1)}, u32[]{:S(2)}, u32[]{:S(2)}) %collective-permute-start.4) | collective-permute-done | bytes 2097184 | tf_op jit(solution)/shard_map/ppermute | solution.py:19
  239.0 4.4 %collective-permute-start.5 = (bf16[2,256,2048]{2,1,0:T(8,128)(2,1)S(1)}, bf16[2,256,2048]{2,1,0:T(8,128)(2,1)}, u32[]{:S(2)}, u32[]{:S(2)}) collective-permute-start(bf16[2,256,2048]{2,1,0:T(8,128)(2,1)S(1)} %collective-permute-done.4), channel_id=1, source_target_pairs={{0,4},{4,8},{8,12},{12,16},{16,20},{20,24},{24,28},{1,5},{5,9},{9,... | collective-permute-start | bytes 6291464 | tf_op jit(solution)/shard_map/ppermute | solution.py:19
  243.4 23.0 %collective-permute-done.5 = bf16[2,256,2048]{2,1,0:T(8,128)(2,1)} collective-permute-done((bf16[2,256,2048]{2,1,0:T(8,128)(2,1)S(1)}, bf16[2,256,2048]{2,1,0:T(8,128)(2,1)}, u32[]{:S(2)}, u32[]{:S(2)}) %collective-permute-start.5) | collective-permute-done | bytes 2097184 | tf_op jit(solution)/shard_map/ppermute | solution.py:19
  266.4 4.7 %collective-permute-start.6 = (bf16[2,256,2048]{2,1,0:T(8,128)(2,1)}, bf16[2,256,2048]{2,1,0:T(8,128)(2,1)}, u32[]{:S(2)}, u32[]{:S(2)}) collective-permute-start(bf16[2,256,2048]{2,1,0:T(8,128)(2,1)} %collective-permute-done.5), channel_id=1, source_target_pairs={{0,4},{4,8},{8,12},{12,16},{16,20},{20,24},{24,28},{1,5},{5,9},{9,... | collective-permute-start | bytes 6291464 | tf_op jit(solution)/shard_map/ppermute | solution.py:19
  271.1 23.0 %collective-permute-done.6 = bf16[2,256,2048]{2,1,0:T(8,128)(2,1)} collective-permute-done((bf16[2,256,2048]{2,1,0:T(8,128)(2,1)}, bf16[2,256,2048]{2,1,0:T(8,128)(2,1)}, u32[]{:S(2)}, u32[]{:S(2)}) %collective-permute-start.6) | collective-permute-done | bytes 2097184 | tf_op jit(solution)/shard_map/ppermute | solution.py:19
  294.1 3.8 pad_maximum_fusion.1
  298.0 3.8 slice_bitcast_fusion
  302.8 82.3 %while.27 = (s32[]{:T(128)}, bf16[4,256,512]{1,2,0:T(8,128)(2,1)}, s32[4]{0:T(128)S(1)}, bf16[4,256,2048]{2,1,0:T(8,128)(2,1)}, bf16[256,2048]{1,0:T(8,128)(2,1)...) while((s32[]{:T(128)}, bf16[4,256,512]{1,2,0:T(8,128)(2,1)}, ...), condition=%wide.region_8.9_spmd.clone, body=%wide.region_5.8_spmd.clone.sunk | while | flops 548537344 | bytes 30692156 | solution.py:79
  304.1 2.6 constant_dynamic-slice_fusion.26
  312.6 4.7 %fusion.167 = (f32[4,256]{1,0:T(4,128)S(1)}, bf16[4,256,1024]{1,2,0:T(8,128)(2,1)S(1)}) fusion(f32[4,256,256]{1,2,0:T(8,128)S(1)} %fusion.163, f32[4,256,256]{1,2,0:T(8,128)} %fusion.164, f32[4,256,256]{1,2,0:T(8,128)} %fusion.165, f32[4,256,256]{1,2,0:T(8,128)S(1)} %fusion.166, pred[256,1024]{0,1:T(8,128)(4,1)S(1)} %and_and_fusion.5), kind=kOutput, calls=%fused_computation.95.clone.1 | output fusion | flops 9438207 | bytes 6557696 | tf_op jit(solution)/shard_map/while/body/eval_jaxpr/sub | solution.py:69
  324.6 2.6 constant_dynamic-slice_fusion.26
  330.4 1.3 fusion.165
  333.2 4.7 %fusion.167 = (f32[4,256]{1,0:T(4,128)S(1)}, bf16[4,256,1024]{1,2,0:T(8,128)(2,1)S(1)}) fusion(f32[4,256,256]{1,2,0:T(8,128)S(1)} %fusion.163, f32[4,256,256]{1,2,0:T(8,128)} %fusion.164, f32[4,256,256]{1,2,0:T(8,128)} %fusion.165, f32[4,256,256]{1,2,0:T(8,128)S(1)} %fusion.166, pred[256,1024]{0,1:T(8,128)(4,1)S(1)} %and_and_fusion.5), kind=kOutput, calls=%fused_computation.95.clone.1 | output fusion | flops 9438207 | bytes 6557696 | tf_op jit(solution)/shard_map/while/body/eval_jaxpr/sub | solution.py:69
  345.2 2.6 constant_dynamic-slice_fusion.26
  351.0 1.3 fusion.165
  353.8 4.7 %fusion.167 = (f32[4,256]{1,0:T(4,128)S(1)}, bf16[4,256,1024]{1,2,0:T(8,128)(2,1)S(1)}) fusion(f32[4,256,256]{1,2,0:T(8,128)S(1)} %fusion.163, f32[4,256,256]{1,2,0:T(8,128)} %fusion.164, f32[4,256,256]{1,2,0:T(8,128)} %fusion.165, f32[4,256,256]{1,2,0:T(8,128)S(1)} %fusion.166, pred[256,1024]{0,1:T(8,128)(4,1)S(1)} %and_and_fusion.5), kind=kOutput, calls=%fused_computation.95.clone.1 | output fusion | flops 9438207 | bytes 6557696 | tf_op jit(solution)/shard_map/while/body/eval_jaxpr/sub | solution.py:69
  365.8 2.6 constant_dynamic-slice_fusion.26
  371.6 1.3 fusion.165
  374.3 4.7 %fusion.167 = (f32[4,256]{1,0:T(4,128)S(1)}, bf16[4,256,1024]{1,2,0:T(8,128)(2,1)S(1)}) fusion(f32[4,256,256]{1,2,0:T(8,128)S(1)} %fusion.163, f32[4,256,256]{1,2,0:T(8,128)} %fusion.164, f32[4,256,256]{1,2,0:T(8,128)} %fusion.165, f32[4,256,256]{1,2,0:T(8,128)S(1)} %fusion.166, pred[256,1024]{0,1:T(8,128)(4,1)S(1)} %and_and_fusion.5), kind=kOutput, calls=%fused_computation.95.clone.1 | output fusion | flops 9438207 | bytes 6557696 | tf_op jit(solution)/shard_map/while/body/eval_jaxpr/sub | solution.py:69
  385.1 2.7 convert_element_type.83
  387.8 2.0 copy.154
  (215 shorter events, 101.0 us)
Async XLA Ops:
  0.0 1.5 copy-start.6
  0.0 62.3 %copy-start.7 = (bf16[1,256,2048]{2,1,0:T(8,128)(2,1)S(1)}, bf16[1,256,2048]{2,1,0:T(8,128)(2,1)}, u32[]{:S(2)}) copy-start(bf16[1,256,2048]{2,1,0:T(8,128)(2,1)} %param.10) | copy-start | bytes 3145732
  1.5 62.1 %copy-start.8 = (s32[4,2048]{1,0:T(4,128)S(1)}, s32[4,2048]{1,0:T(4,128)}, u32[]{:S(2)}) copy-start(s32[4,2048]{1,0:T(4,128)} %param.13) | copy-start | bytes 98308
  1.6 27.5 %collective-permute-start = (bf16[2,256,2048]{2,1,0:T(8,128)(2,1)S(1)}, bf16[2,256,2048]{2,1,0:T(8,128)(2,1)S(1)}, u32[]{:S(2)}, u32[]{:S(2)}) collective-permute-start(bf16[2,256,2048]{2,1,0:T(8,128)(2,1)S(1)} %constant_dynamic-update-slice_fusion.2), channel_id=1, source_target_pairs={{0,4},{4,8},{8,12},{12,16},{16,20},{20,24},{24,28},{1,5},{5,9},{9,... | collective-permute-start | bytes 6291464 | tf_op jit(solution)/shard_map/ppermute | solution.py:19
  29.1 1.3 copy-start.4
  30.5 27.3 %collective-permute-start.1 = (bf16[2,256,2048]{2,1,0:T(8,128)(2,1)S(1)}, bf16[2,256,2048]{2,1,0:T(8,128)(2,1)}, u32[]{:S(2)}, u32[]{:S(2)}) collective-permute-start(bf16[2,256,2048]{2,1,0:T(8,128)(2,1)S(1)} %collective-permute-done), channel_id=1, source_target_pairs={{0,4},{4,8},{8,12},{12,16},{16,20},{20,24},{24,28},{1,5},{5,9},{9,... | collective-permute-start | bytes 6291464 | tf_op jit(solution)/shard_map/ppermute | solution.py:19
  57.8 27.8 %collective-permute-start.2 = (bf16[2,256,2048]{2,1,0:T(8,128)(2,1)}, bf16[2,256,2048]{2,1,0:T(8,128)(2,1)}, u32[]{:S(2)}, u32[]{:S(2)}) collective-permute-start(bf16[2,256,2048]{2,1,0:T(8,128)(2,1)} %collective-permute-done.1), channel_id=1, source_target_pairs={{0,4},{4,8},{8,12},{12,16},{16,20},{20,24},{24,28},{1,5},{5,9},{9,... | collective-permute-start | bytes 6291464 | tf_op jit(solution)/shard_map/ppermute | solution.py:19
  110.3 2.2 copy-start.1
  130.7 2.2 copy-start.1
  151.1 2.2 copy-start.1
  171.5 2.2 copy-start.1
  175.9 2.9 copy-start.9
  175.9 2.9 copy-start.10
  177.4 15.5 %collective-permute-start.3 = (bf16[256,2048]{1,0:T(8,128)(2,1)S(1)}, bf16[256,2048]{1,0:T(8,128)(2,1)S(1)}, u32[]{:S(2)}, u32[]{:S(2)}) collective-permute-start(bf16[256,2048]{1,0:T(8,128)(2,1)S(1)} %copy.153), channel_id=1, source_target_pairs={{3,0},{0,1},{1,2},{2,3},{7,4},{4,5},{5,6},{6,7},{11,8},{8,9},{9,10... | collective-permute-start | bytes 3145736 | tf_op jit(solution)/shard_map/ppermute | solution.py:25
  197.0 1.0 copy-start.2
  198.0 39.6 %collective-permute-start.4 = (bf16[2,256,2048]{2,1,0:T(8,128)(2,1)S(1)}, bf16[2,256,2048]{2,1,0:T(8,128)(2,1)S(1)}, u32[]{:S(2)}, u32[]{:S(2)}) collective-permute-start(bf16[2,256,2048]{2,1,0:T(8,128)(2,1)S(1)} %get-tuple-element.421), channel_id=1, source_target_pairs={{0,4},{4,8},{8,12},{12,16},{16,20},{20,24},{24,28},{1,5},{5,9},{9,... | collective-permute-start | bytes 6291464 | tf_op jit(solution)/shard_map/ppermute | solution.py:19
  237.7 1.3 copy-start.5
  239.0 27.3 %collective-permute-start.5 = (bf16[2,256,2048]{2,1,0:T(8,128)(2,1)S(1)}, bf16[2,256,2048]{2,1,0:T(8,128)(2,1)}, u32[]{:S(2)}, u32[]{:S(2)}) collective-permute-start(bf16[2,256,2048]{2,1,0:T(8,128)(2,1)S(1)} %collective-permute-done.4), channel_id=1, source_target_pairs={{0,4},{4,8},{8,12},{12,16},{16,20},{20,24},{24,28},{1,5},{5,9},{9,... | collective-permute-start | bytes 6291464 | tf_op jit(solution)/shard_map/ppermute | solution.py:19
  266.4 27.8 %collective-permute-start.6 = (bf16[2,256,2048]{2,1,0:T(8,128)(2,1)}, bf16[2,256,2048]{2,1,0:T(8,128)(2,1)}, u32[]{:S(2)}, u32[]{:S(2)}) collective-permute-start(bf16[2,256,2048]{2,1,0:T(8,128)(2,1)} %collective-permute-done.5), channel_id=1, source_target_pairs={{0,4},{4,8},{8,12},{12,16},{16,20},{20,24},{24,28},{1,5},{5,9},{9,... | collective-permute-start | bytes 6291464 | tf_op jit(solution)/shard_map/ppermute | solution.py:19
  319.0 2.2 copy-start
  339.6 2.2 copy-start
  360.2 2.2 copy-start
  380.7 2.2 copy-start
  387.8 2.0 copy-start.3
where the time goes:
time: 394 us; the launch traced here: 391 us
  waiting for transfers between devices  151 us (38%)
  local copies, waits for them, and re-layouts  84.3 us (21%)
  other arithmetic  60.4 us (15%)
  matrix products  49.2 us (12%)
  starting transfers between devices  40.4 us (10%)
  loops' own time  5.96 us (2%)
    ppermute x6, waiting for transfers between devices, from_behind(): return lax.ppermute(block, axis, route)  137 us
    ppermute x6, starting transfers between devices, from_behind(): return lax.ppermute(block, axis, route)  39.1 us
    sub x8, other arithmetic, one_group(): probs = jnp.where(allowed[None], jnp.exp(scores - row_max), 0.0)  37.8 us
    dot_general x32, matrix products, compute(): jnp.einsum('qhd,khd->hqk', query_g, key_tile, preferred_element_type=jnp....  26.9 us
    while x80, local copies, waits for them, and re-layouts  24 us
    dot_general x32, matrix products, compute(): jnp.einsum('hqk,khd->qhd', prob_tile, value_tile, preferred_element_type=...  22.2 us
    slice x8, local copies, waits for them, and re-layouts, one_group(): pieces.append(tile_scores(query_g, key_g[j]))  20.6 us
    ppermute x1, waiting for transfers between devices, shifted(): return lax.ppermute(block, axis, route)  14.1 us
  transfers between devices with their start and end apart: 7, of which 7 were waited for; matrix products, arithmetic and copies ran while one was open for 0% of the time, Pallas kernels for 0%

commit v1 on v0

v1 whole, which is shorter than its diff:
```python
import math

import jax
import jax.numpy as jnp
from jax import lax
from jax.experimental import pallas as pl
from jax.experimental.pallas import tpu as pltpu
from jax.sharding import PartitionSpec as P

HD = 128
HOPS = 3
NEG = -1e30
LOG2E = 1.4426950408889634
MESH = pl.DeviceIdType.MESH


def attend(q, k, v, low, scale):
    rows = q.shape[0]
    span = (HOPS + 1) * rows
    s = lax.dot_general(q, k, (((1,), (1,)), ((), ())), preferred_element_type=jnp.float32)
    row = lax.broadcasted_iota(jnp.int32, (rows, rows), 0)
    col = lax.broadcasted_iota(jnp.int32, (rows, rows), 1)
    new = col <= row
    place = jnp.where(new, col, col - HOPS * rows)
    merged = jnp.where(new, s[:, HOPS * rows :], s[:, :rows])
    parts = [jnp.where(place >= low, merged, NEG)]
    for j in range(1, HOPS):
        parts.append(jnp.where(col + (j - HOPS) * rows >= low, s[:, j * rows : (j + 1) * rows], NEG))
    top = parts[0]
    for part in parts[1:]:
        top = jnp.maximum(top, part)
    m = jnp.max(top, axis=1, keepdims=True)
    probs = [jnp.exp2((part - m) * (scale * LOG2E)) for part in parts]
    total = probs[0]
    for prob in probs[1:]:
        total = total + prob
    l = jnp.sum(total, axis=1, keepdims=True)
    old_p = jnp.where(new, 0.0, probs[0]).astype(jnp.bfloat16)
    new_p = jnp.where(new, probs[0], 0.0).astype(jnp.bfloat16)
    pb = jnp.concatenate([old_p] + [x.astype(jnp.bfloat16) for x in probs[1:]] + [new_p], axis=1)
    out = jnp.dot(pb, v, preferred_element_type=jnp.float32)
    return (out / l).astype(jnp.bfloat16)


def make_kernel(ctx, sections, group, rows, heads_here):
    groups = ctx // group
    pad = HOPS * rows
    width = heads_here * HD

    def kernel(q_in, k_in, v_in, seg, gq, gk, out, qb, kb, vb, fb, xb, nb, k2b, ob,
               in_send, in_recv, z_send, z_recv, o_send, o_recv, *halo):
        c = lax.axis_index("ctx")
        s = lax.axis_index("section")
        grp = c // group
        me = c % group
        base = grp * group
        ahead = lax.rem(s + 1, sections)
        behind = lax.rem(s + sections - 1, sections)
        next_base = lax.rem(grp + 1, groups) * group
        prev_base = lax.rem(grp + groups - 1, groups) * group

        def rows_of(b, count=1):
            return pl.ds(pl.multiple_of(b * rows, rows), count * rows)

        def peer(k):
            return base + lax.rem(me + k, group)

        def cols_of(p, h):
            return pl.ds(pl.multiple_of(lax.rem(p, group) * width + h * HD, HD), HD)

        barrier = pltpu.get_barrier_semaphore()

        def greet(k, carry):
            pl.semaphore_signal(barrier, inc=1, device_id=(peer(k), s), device_id_type=MESH)
            return carry

        lax.fori_loop(1, group, greet, 0)
        pl.semaphore_signal(barrier, inc=1, device_id=(c, ahead), device_id_type=MESH)
        pl.semaphore_signal(barrier, inc=1, device_id=(c, behind), device_id_type=MESH)
        expected = group + 1
        if groups > 1:
            def greet_far(k, carry):
                pl.semaphore_signal(barrier, inc=1, device_id=(next_base + k, s), device_id_type=MESH)
                pl.semaphore_signal(barrier, inc=1, device_id=(prev_base + k, s), device_id_type=MESH)
                return carry

            lax.fori_loop(0, group, greet_far, 0)
            pl.semaphore_signal(barrier, inc=1, device_id=(next_base + me, ahead), device_id_type=MESH)
            pl.semaphore_signal(barrier, inc=1, device_id=(prev_base + me, behind), device_id_type=MESH)
            expected = expected + 2 * group + 2

        ins = (q_in, k_in, v_in)
        bufs = (qb, kb, vb)
        lead = (0, HOPS, HOPS)

        def own_copy(a, h):
            return pltpu.make_async_copy(
                ins[a].at[0, :, cols_of(me, h)], bufs[a].at[h, rows_of(me + lead[a])], in_recv.at[a, h, 0]
            )

        def in_copy(a, h, k, place):
            p = peer(k)
            return pltpu.make_async_remote_copy(
                src_ref=ins[a].at[0, :, cols_of(p, h)],
                dst_ref=bufs[a].at[h, rows_of(place + lead[a])],
                send_sem=in_send.at[a, h, k],
                recv_sem=in_recv.at[a, h, k],
                device_id=(p, s),
                device_id_type=MESH,
            )

        for h in range(heads_here):
            for a in range(3):
                own_copy(a, h).start()
        if groups == 1:
            zero = jnp.zeros((heads_here, pad, HD), jnp.bfloat16)
            kb[:, :pad, :] = zero
            vb[:, :pad, :] = zero
            k2b[:, :pad, :] = zero
            nb[:, :pad, :] = zero
        pl.semaphore_wait(barrier, expected)

        def send_in(t, carry):
            h = t // (group - 1)
            k = 1 + lax.rem(t, group - 1)
            for a in range(3):
                in_copy(a, h, k, me).start()
            return carry

        lax.fori_loop(0, heads_here * (group - 1), send_in, 0)

        if groups > 1:
            hi_send, hi_recv, hz_send, hz_recv = halo

            def halo_in(a, h, k, j):
                return pltpu.make_async_remote_copy(
                    src_ref=ins[a].at[0, :, cols_of(k, h)],
                    dst_ref=bufs[a].at[h, rows_of(j)],
                    send_sem=hi_send.at[a - 1, h, k],
                    recv_sem=hi_recv.at[a - 1, h, j],
                    device_id=(next_base + k, s),
                    device_id_type=MESH,
                )

            def halo_z(h, j, b):
                return pltpu.make_async_remote_copy(
                    src_ref=fb.at[h, rows_of(b)],
                    dst_ref=nb.at[h, rows_of(j)],
                    send_sem=hz_send.at[h, j],
                    recv_sem=hz_recv.at[h, j],
                    device_id=(next_base + me, ahead),
                    device_id_type=MESH,
                )

            @pl.when(me >= group - HOPS)
            def _():
                def send_halo(t, carry):
                    for a in (1, 2):
                        halo_in(a, t // group, lax.rem(t, group), me - (group - HOPS)).start()
                    return carry

                lax.fori_loop(0, heads_here * group, send_halo, 0)

        pos = lax.broadcasted_iota(jnp.int32, (rows, 1), 0)

        def zeros_in(which):
            ids = seg[pl.ds(which, 1), :]
            return jnp.sum(jnp.where(ids == 0, 1.0, 0.0), axis=1, keepdims=True).astype(jnp.int32)

        def low_of(b, cut):
            first = (base + b) * rows
            return jnp.where(pos + first >= cut, cut, 0) - first

        def z_copy(h, b, slot):
            return pltpu.make_async_remote_copy(
                src_ref=fb.at[h, rows_of(b)],
                dst_ref=xb.at[h, rows_of(b)],
                send_sem=z_send.at[h, slot],
                recv_sem=z_recv.at[h, slot],
                device_id=(c, ahead),
                device_id_type=MESH,
            )

        own_cut = zeros_in(s)
        start = lax.rem(me + group - HOPS, group)

        def layer_one(t, carry):
            h = t // group
            i = lax.rem(t, group)

            @pl.when(i == 0)
            def _():
                for a in range(3):
                    own_copy(a, h).wait()

                def arrived(k, inner):
                    for a in range(3):
                        in_copy(a, h, k, lax.rem(me + group - k, group)).wait_recv()
                    return inner

                lax.fori_loop(1, group, arrived, 0)
                if groups > 1:
                    for a in (1, 2):
                        for j in range(HOPS):
                            halo_in(a, h, j, j).wait_recv()

            b = lax.rem(start + i, group)
            fb[h, rows_of(b)] = attend(
                qb[h, rows_of(b)],
                kb[h, rows_of(b, HOPS + 1)],
                vb[h, rows_of(b, HOPS + 1)],
                low_of(b, own_cut),
                1.0 / math.sqrt(HD),
            )
            z_copy(h, b, i).start()
            if groups > 1:
                @pl.when(b >= group - HOPS)
                def _():
                    halo_z(h, b - (group - HOPS), b).start()
            return carry

        lax.fori_loop(0, heads_here * group, layer_one, 0)

        prior_cut = zeros_in(behind)

        def normalize(x):
            x = x.astype(jnp.float32)
            mean = jnp.mean(x * x, axis=1, keepdims=True)
            return (x * lax.rsqrt(mean + 1e-06)).astype(jnp.bfloat16)

        def gained(normed, gain, h):
            g = gain[:, cols_of(me, h)].astype(jnp.float32)
            return (normed.astype(jnp.float32) * g).astype(jnp.bfloat16)

        def take(h, slot):
            b = lax.rem(start + slot, group)
            z_copy(h, b, slot).wait_recv()
            normed = normalize(xb[h, rows_of(b)])
            nb[h, rows_of(b + HOPS)] = normed
            k2b[h, rows_of(b + HOPS)] = gained(normed, gk, h)

        def out_copy(h, k):
            return pltpu.make_async_remote_copy(
                src_ref=ob.at[h, rows_of(lax.rem(me + k, group))],
                dst_ref=out.at[0, :, cols_of(me, h)],
                send_sem=o_send.at[h, k],
                recv_sem=o_recv.at[h, k],
                device_id=(peer(k), s),
                device_id_type=MESH,
            )

        def out_own(h):
            return pltpu.make_async_copy(
                ob.at[h, rows_of(me)], out.at[0, :, cols_of(me, h)], o_recv.at[h, 0]
            )

        def layer_two(t, carry):
            h = t // group
            i = lax.rem(t, group)

            @pl.when(i == 0)
            def _():
                if groups > 1:
                    for j in range(HOPS):
                        halo_z(h, j, j).wait_recv()
                        normed = normalize(nb[h, rows_of(j)])
                        nb[h, rows_of(j)] = normed
                        k2b[h, rows_of(j)] = gained(normed, gk, h)

                def first_ones(slot, inner):
                    take(h, slot)
                    return inner

                lax.fori_loop(0, HOPS, first_ones, 0)

            @pl.when(i < group - HOPS)
            def _():
                take(h, i + HOPS)

            b = lax.rem(me + i, group)
            normed = nb[h, rows_of(b + HOPS)]
            second = attend(
                gained(normed, gq, h),
                k2b[h, rows_of(b, HOPS + 1)],
                nb[h, rows_of(b, HOPS + 1)],
                low_of(b, prior_cut),
                1.0 / HD,
            )
            ob[h, rows_of(b)] = (second.astype(jnp.float32) + normed.astype(jnp.float32)).astype(jnp.bfloat16)

            @pl.when(i == 0)
            def _():
                out_own(h).start()

            @pl.when(i > 0)
            def _():
                out_copy(h, i).start()

            return carry

        lax.fori_loop(0, heads_here * group, layer_two, 0)

        def finish(t, carry):
            h = t // (group - 1)
            k = 1 + lax.rem(t, group - 1)
            for a in range(3):
                in_copy(a, h, k, me).wait_send()
            out_copy(h, k).wait_send()
            p = lax.rem(me + group - k, group)
            pltpu.make_async_remote_copy(
                src_ref=ob.at[h, rows_of(me)],
                dst_ref=out.at[0, :, cols_of(p, h)],
                send_sem=o_send.at[h, k],
                recv_sem=o_recv.at[h, k],
                device_id=(peer(k), s),
                device_id_type=MESH,
            ).wait_recv()
            return carry

        lax.fori_loop(0, heads_here * (group - 1), finish, 0)

        def finish_z(t, carry):
            h = t // group
            i = lax.rem(t, group)
            z_copy(h, lax.rem(start + i, group), i).wait_send()
            return carry

        lax.fori_loop(0, heads_here * group, finish_z, 0)
        for h in range(heads_here):
            out_own(h).wait()
            if groups > 1:
                for j in range(HOPS):
                    halo_z(h, j, group - HOPS + j).wait_send()
        if groups > 1:
            @pl.when(me >= group - HOPS)
            def _():
                def sent_halo(t, carry):
                    for a in (1, 2):
                        halo_in(a, t // group, lax.rem(t, group), me - (group - HOPS)).wait_send()
                    return carry

                lax.fori_loop(0, heads_here * group, sent_halo, 0)

    return kernel


def solution(mesh):
    ctx = mesh.shape["ctx"]
    sections = mesh.shape["section"]
    group = math.gcd(ctx, 8)

    def per_device(queries, keys, values, segments, gain_query, gain_key):
        _, rows, width = queries.shape
        heads_here = width // HD // group
        padded = (group + HOPS) * rows
        bf = jnp.bfloat16
        dma = pltpu.SemaphoreType.DMA
        scratch = [
            pltpu.VMEM((heads_here, group * rows, HD), bf),
            pltpu.VMEM((heads_here, padded, HD), bf),
            pltpu.VMEM((heads_here, padded, HD), bf),
            pltpu.VMEM((heads_here, group * rows, HD), bf),
            pltpu.VMEM((heads_here, group * rows, HD), bf),
            pltpu.VMEM((heads_here, padded, HD), bf),
            pltpu.VMEM((heads_here, padded, HD), bf),
            pltpu.VMEM((heads_here, group * rows, HD), bf),
            dma((3, heads_here, group)),
            dma((3, heads_here, group)),
            dma((heads_here, group)),
            dma((heads_here, group)),
            dma((heads_here, group)),
            dma((heads_here, group)),
        ]
        if ctx > group:
            scratch += [
                dma((2, heads_here, group)),
                dma((2, heads_here, HOPS)),
                dma((heads_here, HOPS)),
                dma((heads_here, HOPS)),
            ]
        hbm = pl.BlockSpec(memory_space=pl.ANY)
        vmem = pl.BlockSpec(memory_space=pltpu.VMEM)
        return pl.pallas_call(
            make_kernel(ctx, sections, group, rows, heads_here),
            out_shape=jax.ShapeDtypeStruct(queries.shape, bf),
            in_specs=[hbm, hbm, hbm, vmem, vmem, vmem],
            out_specs=hbm,
            scratch_shapes=scratch,
            compiler_params=pltpu.CompilerParams(
                collective_id=0, has_side_effects=True, vmem_limit_bytes=48 * 1024 * 1024
            ),
        )(queries, keys, values, segments, gain_query, gain_key)

    return jax.shard_map(
        per_device,
        mesh=mesh,
        in_specs=(
            P("section", "ctx", None),
            P("section", "ctx", None),
            P("section", "ctx", None),
            P(),
            P("section", None),
            P("section", None),
        ),
        out_specs=P("section", "ctx", None),
        check_vma=False,
    )
```

time: 394 us -> 69.2 us (0.18)
  waiting for transfers between devices: 151 us -> 0 us
  local copies, waits for them, and re-layouts: 84.3 us -> 6.8 us
  Pallas kernels: 0 us -> 62 us
  other arithmetic: 60.4 us -> 0 us
  matrix products: 49.2 us -> 0 us
  starting transfers between devices: 40.4 us -> 0 us
  loops' own time: 5.96 us -> 0 us
    ppermute x7 -> x0, waiting for transfers between devices: 151 us -> none  [the longest x6 137 us: from_behind(): return lax.ppermute(block, axis, route)]
    pallas_call x0 -> x1, Pallas kernels: none -> 62 us  [per_device(): pl.pallas_call(make_kernel(ctx, sections, group, rows, heads_here), out_s...]
    dot_general x64 -> x0, matrix products: 49.2 us -> none  [the longest x32 26.9 us: compute(): jnp.einsum('qhd,khd->hqk', query_g, key_tile, preferred_element_type=jnp....]
    ppermute x7 -> x0, starting transfers between devices: 40.4 us -> none  [the longest x6 39.1 us: from_behind(): return lax.ppermute(block, axis, route)]
    sub x8 -> x0, other arithmetic: 37.8 us -> none  [one_group(): probs = jnp.where(allowed[None], jnp.exp(scores - row_max), 0.0)]
    while x80 -> x0, local copies, waits for them, and re-layouts: 24 us -> none
    slice x8 -> x0, local copies, waits for them, and re-layouts: 20.6 us -> none  [one_group(): pieces.append(tile_scores(query_g, key_g[j]))]
    dynamic_slice x22 -> x0, local copies, waits for them, and re-layouts: 13.3 us -> none  [the longest x12 8.33 us: one_group(): lax.dynamic_slice_in_dim(queries, offset, per_group * HD, 1)]
  transfers between devices with their start and end apart: 7 -> 0, of which waited for: 7 -> 0; matrix products, arithmetic and copies ran while one was open for 0% -> 0% of each run, Pallas kernels for 0% -> 0%
where the time goes in v1:
time: 69.2 us; the launch traced here: 68.8 us
  Pallas kernels  62 us (90%)
  local copies, waits for them, and re-layouts  6.8 us (10%)
    pallas_call x1, Pallas kernels, per_device(): pl.pallas_call(make_kernel(ctx, sections, group, rows, heads_here), out_s...  62 us
    unnamed x13, local copies, waits for them, and re-layouts  6.8 us

profile of v1, /device:TPU:1, one launch (start us, length us, event | category | flops | bytes accessed | tf_op | source)
XLA Modules:
  0.0 68.8 jit_solution(10932312219092148660)
XLA Ops:
  0.0 0.0 copy-start
  0.0 1.2 %copy-done = bf16[1,256,2048]{2,1,0:T(8,128)(2,1)S(1)} copy-done((bf16[1,256,2048]{2,1,0:T(8,128)(2,1)S(1)}, bf16[1,256,2048]{2,1,0:T(8,128)(2,1)}, u32[]{:S(2)}) %copy-start) | copy-done | bytes 1048600
  1.2 0.0 copy-start.1
  1.2 1.2 %copy-done.1 = bf16[1,256,2048]{2,1,0:T(8,128)(2,1)S(1)} copy-done((bf16[1,256,2048]{2,1,0:T(8,128)(2,1)S(1)}, bf16[1,256,2048]{2,1,0:T(8,128)(2,1)}, u32[]{:S(2)}) %copy-start.1) | copy-done | bytes 1048600
  2.5 0.0 copy-start.2
  2.5 1.2 %copy-done.2 = bf16[1,256,2048]{2,1,0:T(8,128)(2,1)S(1)} copy-done((bf16[1,256,2048]{2,1,0:T(8,128)(2,1)S(1)}, bf16[1,256,2048]{2,1,0:T(8,128)(2,1)}, u32[]{:S(2)}) %copy-start.2) | copy-done | bytes 1048600
  3.7 0.0 copy-start.3
  3.7 0.8 %copy-done.3 = s32[4,2048]{1,0:T(4,128)S(1)} copy-done((s32[4,2048]{1,0:T(4,128)S(1)}, s32[4,2048]{1,0:T(4,128)}, u32[]{:S(2)}) %copy-start.3) | copy-done | bytes 32792
  4.4 0.0 copy-start.4
  4.4 0.7 %copy-done.4 = bf16[1,2048]{1,0:T(2,128)(2,1)S(1)} copy-done((bf16[1,2048]{1,0:T(2,128)(2,1)S(1)}, bf16[1,2048]{1,0:T(2,128)(2,1)}, u32[]{:S(2)}) %copy-start.4) | copy-done | bytes 4120
  5.1 0.0 copy-start.5
  5.1 0.7 %copy-done.5 = bf16[1,2048]{1,0:T(2,128)(2,1)S(1)} copy-done((bf16[1,2048]{1,0:T(2,128)(2,1)S(1)}, bf16[1,2048]{1,0:T(2,128)(2,1)}, u32[]{:S(2)}) %copy-start.5) | copy-done | bytes 4120
  5.8 62.0 %shard_map.64 = bf16[1,256,2048]{2,1,0:T(8,128)(2,1)S(1)} custom-call(bf16[1,256,2048]{2,1,0:T(8,128)(2,1)S(1)} %copy-done, bf16[1,256,2048]{2,1,0:T(8,128)(2,1)S(1)} %copy-done.1, bf16[1,256,2048]{2,1,0:T(8,128)(2,1)S(1)} %copy-done.2, s32[4,2048]{1,0:T(4,128)S(1)} %copy-done.3, bf16[1,2048]{1,0:T(2,128)(2,1)S(1)} %copy-done.4, bf16[1,2048]{1,0:T(2,128)(2,1)S(1)} %copy-done.5), custom_call_target="tpu_custom_call" | custom-call | tf_op jit(solution)/shard_map/pallas_call | solution.py:383
  67.8 1.0 %copy.8 = bf16[1,256,2048]{2,1,0:T(8,128)(2,1)} copy(bf16[1,256,2048]{2,1,0:T(8,128)(2,1)S(1)} %shard_map.64) | data formatting | bytes 2097152
Async XLA Ops:
  0.0 1.2 %copy-start = (bf16[1,256,2048]{2,1,0:T(8,128)(2,1)S(1)}, bf16[1,256,2048]{2,1,0:T(8,128)(2,1)}, u32[]{:S(2)}) copy-start(bf16[1,256,2048]{2,1,0:T(8,128)(2,1)} %q_in.1) | copy-start | bytes 3145732
  1.2 1.2 %copy-start.1 = (bf16[1,256,2048]{2,1,0:T(8,128)(2,1)S(1)}, bf16[1,256,2048]{2,1,0:T(8,128)(2,1)}, u32[]{:S(2)}) copy-start(bf16[1,256,2048]{2,1,0:T(8,128)(2,1)} %k_in.1) | copy-start | bytes 3145732
  2.5 1.2 %copy-start.2 = (bf16[1,256,2048]{2,1,0:T(8,128)(2,1)S(1)}, bf16[1,256,2048]{2,1,0:T(8,128)(2,1)}, u32[]{:S(2)}) copy-start(bf16[1,256,2048]{2,1,0:T(8,128)(2,1)} %v_in.1) | copy-start | bytes 3145732
  3.7 0.8 %copy-start.3 = (s32[4,2048]{1,0:T(4,128)S(1)}, s32[4,2048]{1,0:T(4,128)}, u32[]{:S(2)}) copy-start(s32[4,2048]{1,0:T(4,128)} %seg.1) | copy-start | bytes 98308
  4.4 0.7 %copy-start.4 = (bf16[1,2048]{1,0:T(2,128)(2,1)S(1)}, bf16[1,2048]{1,0:T(2,128)(2,1)}, u32[]{:S(2)}) copy-start(bf16[1,2048]{1,0:T(2,128)(2,1)} %gq.1) | copy-start | bytes 12292
  5.1 0.7 %copy-start.5 = (bf16[1,2048]{1,0:T(2,128)(2,1)S(1)}, bf16[1,2048]{1,0:T(2,128)(2,1)}, u32[]{:S(2)}) copy-start(bf16[1,2048]{1,0:T(2,128)(2,1)} %gk.1) | copy-start | bytes 12292

commit v2 on v1

--- a/solution.py
+++ b/solution.py
@@ -14,10 +14,12 @@
 MESH = pl.DeviceIdType.MESH
 
 
-def attend(q, k, v, low, scale):
-    rows = q.shape[0]
-    span = (HOPS + 1) * rows
-    s = lax.dot_general(q, k, (((1,), (1,)), ((), ())), preferred_element_type=jnp.float32)
+def score_of(q, k):
+    return lax.dot_general(q, k, (((1,), (1,)), ((), ())), preferred_element_type=jnp.float32)
+
+
+def weights_of(s, low, scale, shift):
+    rows = s.shape[0]
     row = lax.broadcasted_iota(jnp.int32, (rows, rows), 0)
     col = lax.broadcasted_iota(jnp.int32, (rows, rows), 1)
     new = col <= row
@@ -26,20 +28,30 @@
     parts = [jnp.where(place >= low, merged, NEG)]
     for j in range(1, HOPS):
         parts.append(jnp.where(col + (j - HOPS) * rows >= low, s[:, j * rows : (j + 1) * rows], NEG))
-    top = parts[0]
-    for part in parts[1:]:
-        top = jnp.maximum(top, part)
-    m = jnp.max(top, axis=1, keepdims=True)
-    probs = [jnp.exp2((part - m) * (scale * LOG2E)) for part in parts]
+    if shift:
+        top = parts[0]
+        for part in parts[1:]:
+            top = jnp.maximum(top, part)
+        m = jnp.max(top, axis=1, keepdims=True)
+        parts = [part - m for part in parts]
+    probs = [jnp.exp2(part * (scale * LOG2E)) for part in parts]
     total = probs[0]
     for prob in probs[1:]:
         total = total + prob
     l = jnp.sum(total, axis=1, keepdims=True)
     old_p = jnp.where(new, 0.0, probs[0]).astype(jnp.bfloat16)
     new_p = jnp.where(new, probs[0], 0.0).astype(jnp.bfloat16)
-    pb = jnp.concatenate([old_p] + [x.astype(jnp.bfloat16) for x in probs[1:]] + [new_p], axis=1)
-    out = jnp.dot(pb, v, preferred_element_type=jnp.float32)
-    return (out / l).astype(jnp.bfloat16)
+    return jnp.concatenate([old_p] + [x.astype(jnp.bfloat16) for x in probs[1:]] + [new_p], axis=1), l
+
+
+def attend_all(tiles, scale, shift):
+    scores = [score_of(q, k) for q, k, _, _ in tiles]
+    outs = []
+    for s, (_, _, v, low) in zip(scores, tiles):
+        pb, l = weights_of(s, low, scale, shift)
+        out = jnp.dot(pb, v, preferred_element_type=jnp.float32)
+        outs.append((out / l).astype(jnp.bfloat16))
+    return outs
 
 
 def make_kernel(ctx, sections, group, rows, heads_here):
@@ -47,8 +59,8 @@
     pad = HOPS * rows
     width = heads_here * HD
 
-    def kernel(q_in, k_in, v_in, seg, gq, gk, out, qb, kb, vb, fb, xb, nb, k2b, ob,
-               in_send, in_recv, z_send, z_recv, o_send, o_recv, *halo):
+    def kernel(q_in, k_in, v_in, seg_in, gq_in, gk_in, out, qb, kb, vb, fb, xb, nb, k2b, ob, seg, gq, gk,
+               small, in_send, in_recv, z_send, z_recv, o_send, o_recv, *halo):
         c = lax.axis_index("ctx")
         s = lax.axis_index("section")
         grp = c // group
@@ -109,6 +121,12 @@
                 device_id_type=MESH,
             )
 
+        smalls = [
+            pltpu.make_async_copy(src, dst, small.at[j])
+            for j, (src, dst) in enumerate(((seg_in, seg), (gq_in, gq), (gk_in, gk)))
+        ]
+        for copy in smalls:
+            copy.start()
         for h in range(heads_here):
             for a in range(3):
                 own_copy(a, h).start()
@@ -123,11 +141,19 @@
         def send_in(t, carry):
             h = t // (group - 1)
             k = 1 + lax.rem(t, group - 1)
+
+            @pl.when(h > 0)
+            def _():
+                for a in range(3):
+                    in_copy(a, h - 1, k, me).wait_send()
+
             for a in range(3):
                 in_copy(a, h, k, me).start()
             return carry
 
         lax.fori_loop(0, heads_here * (group - 1), send_in, 0)
+        for copy in smalls:
+            copy.wait()
 
         if groups > 1:
             hi_send, hi_recv, hz_send, hz_recv = halo
@@ -185,8 +211,8 @@
         start = lax.rem(me + group - HOPS, group)
 
         def layer_one(t, carry):
-            h = t // group
-            i = lax.rem(t, group)
+            h = t // (group // 2)
+            i = 2 * lax.rem(t, group // 2)
 
             @pl.when(i == 0)
             def _():
@@ -204,22 +230,30 @@
                         for j in range(HOPS):
                             halo_in(a, h, j, j).wait_recv()
 
-            b = lax.rem(start + i, group)
-            fb[h, rows_of(b)] = attend(
-                qb[h, rows_of(b)],
-                kb[h, rows_of(b, HOPS + 1)],
-                vb[h, rows_of(b, HOPS + 1)],
-                low_of(b, own_cut),
+            tiles = [lax.rem(start + i + j, group) for j in range(2)]
+            results = attend_all(
+                [
+                    (
+                        qb[h, rows_of(b)],
+                        kb[h, rows_of(b, HOPS + 1)],
+                        vb[h, rows_of(b, HOPS + 1)],
+                        low_of(b, own_cut),
+                    )
+                    for b in tiles
+                ],
                 1.0 / math.sqrt(HD),
-            )
-            z_copy(h, b, i).start()
-            if groups > 1:
-                @pl.when(b >= group - HOPS)
-                def _():
-                    halo_z(h, b - (group - HOPS), b).start()
-            return carry
-
-        lax.fori_loop(0, heads_here * group, layer_one, 0)
+                True,
+            )
+            for j, (b, result) in enumerate(zip(tiles, results)):
+                fb[h, rows_of(b)] = result
+                z_copy(h, b, i + j).start()
+                if groups > 1:
+                    @pl.when(b >= group - HOPS)
+                    def _():
+                        halo_z(h, b - (group - HOPS), b).start()
+            return carry
+
+        lax.fori_loop(0, heads_here * (group // 2), layer_one, 0)
 
         prior_cut = zeros_in(behind)
 
@@ -255,8 +289,8 @@
             )
 
         def layer_two(t, carry):
-            h = t // group
-            i = lax.rem(t, group)
+            h = t // (group // 2)
+            i = 2 * lax.rem(t, group // 2)
 
             @pl.when(i == 0)
             def _():
@@ -273,20 +307,29 @@
 
                 lax.fori_loop(0, HOPS, first_ones, 0)
 
-            @pl.when(i < group - HOPS)
-            def _():
-                take(h, i + HOPS)
-
-            b = lax.rem(me + i, group)
-            normed = nb[h, rows_of(b + HOPS)]
-            second = attend(
-                gained(normed, gq, h),
-                k2b[h, rows_of(b, HOPS + 1)],
-                nb[h, rows_of(b, HOPS + 1)],
-                low_of(b, prior_cut),
+            for j in range(2):
+                @pl.when(i + j < group - HOPS)
+                def _():
+                    take(h, i + j + HOPS)
+
+            tiles = [lax.rem(me + i + j, group) for j in range(2)]
+            normed = [nb[h, rows_of(b + HOPS)] for b in tiles]
+            results = attend_all(
+                [
+                    (
+                        gained(own, gq, h),
+                        k2b[h, rows_of(b, HOPS + 1)],
+                        nb[h, rows_of(b, HOPS + 1)],
+                        low_of(b, prior_cut),
+                    )
+                    for b, own in zip(tiles, normed)
+                ],
                 1.0 / HD,
-            )
-            ob[h, rows_of(b)] = (second.astype(jnp.float32) + normed.astype(jnp.float32)).astype(jnp.bfloat16)
+                False,
+            )
+            for b, own, second in zip(tiles, normed, results):
+                mixed = second.astype(jnp.float32) + own.astype(jnp.float32)
+                ob[h, rows_of(b)] = mixed.astype(jnp.bfloat16)
 
             @pl.when(i == 0)
             def _():
@@ -296,15 +339,19 @@
             def _():
                 out_copy(h, i).start()
 
-            return carry
-
-        lax.fori_loop(0, heads_here * group, layer_two, 0)
+            out_copy(h, i + 1).start()
+            return carry
+
+        lax.fori_loop(0, heads_here * (group // 2), layer_two, 0)
 
         def finish(t, carry):
             h = t // (group - 1)
             k = 1 + lax.rem(t, group - 1)
-            for a in range(3):
-                in_copy(a, h, k, me).wait_send()
+            @pl.when(h == heads_here - 1)
+            def _():
+                for a in range(3):
+                    in_copy(a, h, k, me).wait_send()
+
             out_copy(h, k).wait_send()
             p = lax.rem(me + group - k, group)
             pltpu.make_async_remote_copy(
@@ -364,6 +411,10 @@
             pltpu.VMEM((heads_here, padded, HD), bf),
             pltpu.VMEM((heads_here, padded, HD), bf),
             pltpu.VMEM((heads_here, group * rows, HD), bf),
+            pltpu.VMEM(segments.shape, segments.dtype),
+            pltpu.VMEM(gain_query.shape, bf),
+            pltpu.VMEM(gain_key.shape, bf),
+            dma((3,)),
             dma((3, heads_here, group)),
             dma((3, heads_here, group)),
             dma((heads_here, group)),
@@ -379,15 +430,14 @@
                 dma((heads_here, HOPS)),
             ]
         hbm = pl.BlockSpec(memory_space=pl.ANY)
-        vmem = pl.BlockSpec(memory_space=pltpu.VMEM)
         return pl.pallas_call(
             make_kernel(ctx, sections, group, rows, heads_here),
             out_shape=jax.ShapeDtypeStruct(queries.shape, bf),
-            in_specs=[hbm, hbm, hbm, vmem, vmem, vmem],
+            in_specs=[hbm] * 6,
             out_specs=hbm,
             scratch_shapes=scratch,
             compiler_params=pltpu.CompilerParams(
-                collective_id=0, has_side_effects=True, vmem_limit_bytes=48 * 1024 * 1024
+                collective_id=0, has_side_effects=True, vmem_limit_bytes=60 * 1024 * 1024
             ),
         )(queries, keys, values, segments, gain_query, gain_key)
 

time: 69.2 us -> 62.4 us (0.902)
  local copies, waits for them, and re-layouts: 6.8 us -> 2.3 us
  Pallas kernels: 62 us -> 59.8 us
    unnamed x13 -> x1, local copies, waits for them, and re-layouts: 6.8 us -> 2.3 us
    pallas_call x1, Pallas kernels: 62 us -> 59.8 us  [per_device(): pl.pallas_call(make_kernel(ctx, sections, group, rows, heads_here), out_s...]
where the time goes in v2:
time: 62.4 us; the launch traced here: 62.1 us
  Pallas kernels  59.8 us (96%)
  local copies, waits for them, and re-layouts  2.3 us (4%)
    pallas_call x1, Pallas kernels, per_device(): pl.pallas_call(make_kernel(ctx, sections, group, rows, heads_here), out_s...  59.8 us
    unnamed x1, local copies, waits for them, and re-layouts  2.3 us

profile of v2, /device:TPU:1, one launch (start us, length us, event | category | flops | bytes accessed | tf_op | source)
XLA Modules:
  0.0 62.1 jit_solution(10642182079746931996)
XLA Ops:
  0.0 59.8 %shard_map.64 = bf16[1,256,2048]{2,1,0:T(8,128)(2,1)} custom-call(bf16[1,256,2048]{2,1,0:T(8,128)(2,1)} %q_in.1, bf16[1,256,2048]{2,1,0:T(8,128)(2,1)} %k_in.1, bf16[1,256,2048]{2,1,0:T(8,128)(2,1)} %v_in.1, s32[4,2048]{1,0:T(4,128)} %seg_in.1, bf16[1,2048]{1,0:T(2,128)(2,1)} %gq_in.1, bf16[1,2048]{1,0:T(2,128)(2,1)} %gk_in.1), custom_call_target="tpu_custom_call" | custom-call | tf_op jit(solution)/shard_map/pallas_call | solution.py:433
  59.8 2.3 %copy.8 = bf16[1,256,2048]{2,1,0:T(8,128)(2,1)} copy(bf16[1,256,2048]{2,1,0:T(8,128)(2,1)} %shard_map.64) | data formatting | bytes 2097152

commit v3 on v2

--- a/solution.py
+++ b/solution.py
@@ -138,20 +138,25 @@
             nb[:, :pad, :] = zero
         pl.semaphore_wait(barrier, expected)
 
+        half = group // 2
+
         def send_in(t, carry):
-            h = t // (group - 1)
-            k = 1 + lax.rem(t, group - 1)
-
-            @pl.when(h > 0)
-            def _():
+            h = t // group
+            k = lax.rem(t // half + me, 2) + 2 * lax.rem(t, half)
+
+            @pl.when(k > 0)
+            def _():
+                @pl.when(h > 0)
+                def _():
+                    for a in range(3):
+                        in_copy(a, h - 1, k, me).wait_send()
+
                 for a in range(3):
-                    in_copy(a, h - 1, k, me).wait_send()
-
-            for a in range(3):
-                in_copy(a, h, k, me).start()
+                    in_copy(a, h, k, me).start()
+
             return carry
 
-        lax.fori_loop(0, heads_here * (group - 1), send_in, 0)
+        lax.fori_loop(0, heads_here * group, send_in, 0)
         for copy in smalls:
             copy.wait()
 
@@ -210,9 +215,8 @@
         own_cut = zeros_in(s)
         start = lax.rem(me + group - HOPS, group)
 
-        def layer_one(t, carry):
-            h = t // (group // 2)
-            i = 2 * lax.rem(t, group // 2)
+        def layer_one(t, h):
+            i = 2 * t
 
             @pl.when(i == 0)
             def _():
@@ -251,9 +255,7 @@
                     @pl.when(b >= group - HOPS)
                     def _():
                         halo_z(h, b - (group - HOPS), b).start()
-            return carry
-
-        lax.fori_loop(0, heads_here * (group // 2), layer_one, 0)
+            return h
 
         prior_cut = zeros_in(behind)
 
@@ -288,9 +290,8 @@
                 ob.at[h, rows_of(me)], out.at[0, :, cols_of(me, h)], o_recv.at[h, 0]
             )
 
-        def layer_two(t, carry):
-            h = t // (group // 2)
-            i = 2 * lax.rem(t, group // 2)
+        def layer_two(t, h):
+            i = 2 * t
 
             @pl.when(i == 0)
             def _():
@@ -340,9 +341,14 @@
                 out_copy(h, i).start()
 
             out_copy(h, i + 1).start()
+            return h
+
+        def both_layers(h, carry):
+            lax.fori_loop(0, half, layer_one, h)
+            lax.fori_loop(0, half, layer_two, h)
             return carry
 
-        lax.fori_loop(0, heads_here * (group // 2), layer_two, 0)
+        lax.fori_loop(0, heads_here, both_layers, 0)
 
         def finish(t, carry):
             h = t // (group - 1)
@@ -429,12 +435,11 @@
                 dma((heads_here, HOPS)),
                 dma((heads_here, HOPS)),
             ]
-        hbm = pl.BlockSpec(memory_space=pl.ANY)
         return pl.pallas_call(
             make_kernel(ctx, sections, group, rows, heads_here),
             out_shape=jax.ShapeDtypeStruct(queries.shape, bf),
-            in_specs=[hbm] * 6,
-            out_specs=hbm,
+            in_specs=[pl.BlockSpec(memory_space=pltpu.HBM)] * 6,
+            out_specs=pl.BlockSpec(memory_space=pl.ANY),
             scratch_shapes=scratch,
             compiler_params=pltpu.CompilerParams(
                 collective_id=0, has_side_effects=True, vmem_limit_bytes=60 * 1024 * 1024

time: 62.4 us -> 64.6 us (1.035)
  Pallas kernels: 59.8 us -> 62.1 us
    pallas_call x1, Pallas kernels: 59.8 us -> 62.1 us  [per_device(): pl.pallas_call(make_kernel(ctx, sections, group, rows, heads_here), out_s...]
where the time goes in v3:
time: 64.6 us; the launch traced here: 64.4 us
  Pallas kernels  62.1 us (96%)
  local copies, waits for them, and re-layouts  2.3 us (4%)
    pallas_call x1, Pallas kernels, per_device(): pl.pallas_call(make_kernel(ctx, sections, group, rows, heads_here), out_s...  62.1 us
    unnamed x1, local copies, waits for them, and re-layouts  2.3 us

profile of v3, /device:TPU:1, one launch (start us, length us, event | category | flops | bytes accessed | tf_op | source)
XLA Modules:
  0.0 64.4 jit_solution(13516266853921001556)
XLA Ops:
  0.0 62.1 %shard_map.64 = bf16[1,256,2048]{2,1,0:T(8,128)(2,1)} custom-call(bf16[1,256,2048]{2,1,0:T(8,128)(2,1)} %q_in.1, bf16[1,256,2048]{2,1,0:T(8,128)(2,1)} %k_in.1, bf16[1,256,2048]{2,1,0:T(8,128)(2,1)} %v_in.1, s32[4,2048]{1,0:T(4,128)} %seg_in.1, bf16[1,2048]{1,0:T(2,128)(2,1)} %gq_in.1, bf16[1,2048]{1,0:T(2,128)(2,1)} %gk_in.1), custom_call_target="tpu_custom_call" | custom-call | tf_op jit(solution)/shard_map/pallas_call | solution.py:438
  62.1 2.3 %copy.8 = bf16[1,256,2048]{2,1,0:T(8,128)(2,1)} copy(bf16[1,256,2048]{2,1,0:T(8,128)(2,1)} %shard_map.64) | data formatting | bytes 2097152

commit v4 on v3

--- a/solution.py
+++ b/solution.py
@@ -146,11 +146,6 @@
 
             @pl.when(k > 0)
             def _():
-                @pl.when(h > 0)
-                def _():
-                    for a in range(3):
-                        in_copy(a, h - 1, k, me).wait_send()
-
                 for a in range(3):
                     in_copy(a, h, k, me).start()
 
@@ -343,21 +338,21 @@
             out_copy(h, i + 1).start()
             return h
 
-        def both_layers(h, carry):
-            lax.fori_loop(0, half, layer_one, h)
-            lax.fori_loop(0, half, layer_two, h)
-            return carry
-
-        lax.fori_loop(0, heads_here, both_layers, 0)
+        def all_tiles(layer):
+            def one_head(h, carry):
+                lax.fori_loop(0, half, layer, h)
+                return carry
+
+            lax.fori_loop(0, heads_here, one_head, 0)
+
+        all_tiles(layer_one)
+        all_tiles(layer_two)
 
         def finish(t, carry):
             h = t // (group - 1)
             k = 1 + lax.rem(t, group - 1)
-            @pl.when(h == heads_here - 1)
-            def _():
-                for a in range(3):
-                    in_copy(a, h, k, me).wait_send()
-
+            for a in range(3):
+                in_copy(a, h, k, me).wait_send()
             out_copy(h, k).wait_send()
             p = lax.rem(me + group - k, group)
             pltpu.make_async_remote_copy(

time: 64.6 us -> 60.3 us (0.933)
  Pallas kernels: 62.1 us -> 57.9 us
    pallas_call x1, Pallas kernels: 62.1 us -> 57.9 us  [per_device(): pl.pallas_call(make_kernel(ctx, sections, group, rows, heads_here), out_s...]
where the time goes in v4:
time: 60.3 us; the launch traced here: 60.2 us
  Pallas kernels  57.9 us (96%)
  local copies, waits for them, and re-layouts  2.3 us (4%)
    pallas_call x1, Pallas kernels, per_device(): pl.pallas_call(make_kernel(ctx, sections, group, rows, heads_here), out_s...  57.9 us
    unnamed x1, local copies, waits for them, and re-layouts  2.3 us

profile of v4, /device:TPU:1, one launch (start us, length us, event | category | flops | bytes accessed | tf_op | source)
XLA Modules:
  0.0 60.2 jit_solution(7469968416163951348)
XLA Ops:
  0.0 57.9 %shard_map.64 = bf16[1,256,2048]{2,1,0:T(8,128)(2,1)} custom-call(bf16[1,256,2048]{2,1,0:T(8,128)(2,1)} %q_in.1, bf16[1,256,2048]{2,1,0:T(8,128)(2,1)} %k_in.1, bf16[1,256,2048]{2,1,0:T(8,128)(2,1)} %v_in.1, s32[4,2048]{1,0:T(4,128)} %seg_in.1, bf16[1,2048]{1,0:T(2,128)(2,1)} %gq_in.1, bf16[1,2048]{1,0:T(2,128)(2,1)} %gk_in.1), custom_call_target="tpu_custom_call" | custom-call | tf_op jit(solution)/shard_map/pallas_call | solution.py:433
  57.9 2.3 %copy.8 = bf16[1,256,2048]{2,1,0:T(8,128)(2,1)} copy(bf16[1,256,2048]{2,1,0:T(8,128)(2,1)} %shard_map.64) | data formatting | bytes 2097152

commit v5 on v3

--- a/solution.py
+++ b/solution.py
@@ -146,11 +146,6 @@
 
             @pl.when(k > 0)
             def _():
-                @pl.when(h > 0)
-                def _():
-                    for a in range(3):
-                        in_copy(a, h - 1, k, me).wait_send()
-
                 for a in range(3):
                     in_copy(a, h, k, me).start()
 
@@ -353,11 +348,8 @@
         def finish(t, carry):
             h = t // (group - 1)
             k = 1 + lax.rem(t, group - 1)
-            @pl.when(h == heads_here - 1)
-            def _():
-                for a in range(3):
-                    in_copy(a, h, k, me).wait_send()
-
+            for a in range(3):
+                in_copy(a, h, k, me).wait_send()
             out_copy(h, k).wait_send()
             p = lax.rem(me + group - k, group)
             pltpu.make_async_remote_copy(

time: 64.6 us -> 59.2 us (0.916)
  Pallas kernels: 62.1 us -> 56.7 us
    pallas_call x1, Pallas kernels: 62.1 us -> 56.7 us  [per_device(): pl.pallas_call(make_kernel(ctx, sections, group, rows, heads_here), out_s...]
where the time goes in v5:
time: 59.2 us; the launch traced here: 59 us
  Pallas kernels  56.7 us (96%)
  local copies, waits for them, and re-layouts  2.3 us (4%)
    pallas_call x1, Pallas kernels, per_device(): pl.pallas_call(make_kernel(ctx, sections, group, rows, heads_here), out_s...  56.7 us
    unnamed x1, local copies, waits for them, and re-layouts  2.3 us

profile of v5, /device:TPU:1, one launch (start us, length us, event | category | flops | bytes accessed | tf_op | source)
XLA Modules:
  0.0 59.0 jit_solution(12267271671128759386)
XLA Ops:
  0.0 56.7 %shard_map.64 = bf16[1,256,2048]{2,1,0:T(8,128)(2,1)} custom-call(bf16[1,256,2048]{2,1,0:T(8,128)(2,1)} %q_in.1, bf16[1,256,2048]{2,1,0:T(8,128)(2,1)} %k_in.1, bf16[1,256,2048]{2,1,0:T(8,128)(2,1)} %v_in.1, s32[4,2048]{1,0:T(4,128)} %seg_in.1, bf16[1,2048]{1,0:T(2,128)(2,1)} %gq_in.1, bf16[1,2048]{1,0:T(2,128)(2,1)} %gk_in.1), custom_call_target="tpu_custom_call" | custom-call | tf_op jit(solution)/shard_map/pallas_call | solution.py:430
  56.7 2.3 %copy.8 = bf16[1,256,2048]{2,1,0:T(8,128)(2,1)} copy(bf16[1,256,2048]{2,1,0:T(8,128)(2,1)} %shard_map.64) | data formatting | bytes 2097152

commit v6 on v5

--- a/solution.py
+++ b/solution.py
@@ -27,7 +27,7 @@
     merged = jnp.where(new, s[:, HOPS * rows :], s[:, :rows])
     parts = [jnp.where(place >= low, merged, NEG)]
     for j in range(1, HOPS):
-        parts.append(jnp.where(col + (j - HOPS) * rows >= low, s[:, j * rows : (j + 1) * rows], NEG))
+        parts.append(jnp.where(col >= low + (HOPS - j) * rows, s[:, j * rows : (j + 1) * rows], NEG))
     if shift:
         top = parts[0]
         for part in parts[1:]:

time: 59.2 us -> 59.3 us (level)
  no operation moved by 1% of the time
where the time goes in v6:
time: 59.3 us; the launch traced here: 59.1 us
  Pallas kernels  56.8 us (96%)
  local copies, waits for them, and re-layouts  2.3 us (4%)
    pallas_call x1, Pallas kernels, per_device(): pl.pallas_call(make_kernel(ctx, sections, group, rows, heads_here), out_s...  56.8 us
    unnamed x1, local copies, waits for them, and re-layouts  2.3 us

profile of v6, /device:TPU:1, one launch (start us, length us, event | category | flops | bytes accessed | tf_op | source)
XLA Modules:
  0.0 59.1 jit_solution(1878640809286997630)
XLA Ops:
  0.0 56.8 %shard_map.64 = bf16[1,256,2048]{2,1,0:T(8,128)(2,1)} custom-call(bf16[1,256,2048]{2,1,0:T(8,128)(2,1)} %q_in.1, bf16[1,256,2048]{2,1,0:T(8,128)(2,1)} %k_in.1, bf16[1,256,2048]{2,1,0:T(8,128)(2,1)} %v_in.1, s32[4,2048]{1,0:T(4,128)} %seg_in.1, bf16[1,2048]{1,0:T(2,128)(2,1)} %gq_in.1, bf16[1,2048]{1,0:T(2,128)(2,1)} %gk_in.1), custom_call_target="tpu_custom_call" | custom-call | tf_op jit(solution)/shard_map/pallas_call | solution.py:430
  56.8 2.3 %copy.8 = bf16[1,256,2048]{2,1,0:T(8,128)(2,1)} copy(bf16[1,256,2048]{2,1,0:T(8,128)(2,1)} %shard_map.64) | data formatting | bytes 2097152
